TPU v7x, 512 devices: a whole 4x8x8 slice. The times are simulated.
512 devices in a mesh: gx: 8 (over z_lo, x), gy: 8 (over y), gz: 8 (over z_hi, core).
Axes of the slice: x: 4, y: 8, z: 8 (z_hi: 4, z_lo: 2; z = z_hi * 2 + z_lo), core: 2. Of those that a mesh axis runs over, the one named last changes fastest.
Arguments:
- grad_act: bfloat16 [3072, 24576], P('gz', ('gy', 'gx')), may hold values from -6 to 6
- pre_act: bfloat16 [3072, 24576], P('gz', ('gy', 'gx')), may hold values from -8 to 8
- inputs: bfloat16 [3072, 6144], P('gz', 'gx'), may hold values from -0.109375 to 0.109375
- weight: bfloat16 [6144, 24576], P('gx', ('gy', 'gz')), may hold values from -0.21875 to 0.21875
Outputs:
- grad_inputs: bfloat16 [3072, 6144], P('gz', ('gx', 'gy'))
- grad_weight: bfloat16 [6144, 24576], P('gx', ('gy', 'gz'))
All inputs are finite; a program needn't handle non-finite values.
Results may differ from a plain program's by a relative error of at most 0.0058.
Values may be sent and summed in bfloat16 or wider, within the bound.
A program may use at most 64 MiB of HBM per device.

v0:
```python
import jax
import jax.numpy as jnp
from jax import lax
from jax.sharding import PartitionSpec as P

root_half = 0.7071067811865476
inv_root_tau = 0.3989422804014327


def gelu_grad(grad_act, pre_act):
    value = pre_act.astype(jnp.float32)
    cdf = 0.5 * (1.0 + jax.scipy.special.erf(value * root_half))
    pdf = jnp.exp(-0.5 * value * value) * inv_root_tau
    return (grad_act.astype(jnp.float32) * (cdf + value * pdf)).astype(jnp.bfloat16)


def contract_last(left, right):
    return lax.dot_general(
        left, right, (((1,), (1,)), ((), ())), preferred_element_type=jnp.float32
    )


def contract_first(left, right):
    return lax.dot_general(
        left, right, (((0,), (0,)), ((), ())), preferred_element_type=jnp.float32
    )


def shards(grad_act, pre_act, inputs, weight):
    grad_hidden = gelu_grad(grad_act, pre_act)
    feat_rows = inputs.shape[1]
    width_y = grad_hidden.shape[1] * lax.axis_size("gx")
    groups = lax.axis_size("gz")
    width_z = width_y // groups
    whole_weight = lax.all_gather(weight, "gz", axis=1, tiled=True)
    piece = lax.all_gather(grad_hidden, "gx", axis=1, tiled=True)
    acc_inputs = contract_last(piece, whole_weight)
    part = contract_first(inputs, piece).astype(jnp.bfloat16)
    kept = part
    acc_inputs, kept = (acc_inputs, kept)
    stacked = kept.reshape(feat_rows, groups, width_z)
    received = lax.all_to_all(stacked, "gz", split_axis=1, concat_axis=1, tiled=True)
    grad_weight = jnp.sum(received, axis=1, dtype=jnp.float32).astype(jnp.bfloat16)
    grad_inputs = lax.psum_scatter(acc_inputs, "gy", scatter_dimension=1, tiled=True).astype(
        jnp.bfloat16
    )
    return (grad_inputs, grad_weight)


def solution(mesh):
    return jax.shard_map(
        shards,
        mesh=mesh,
        in_specs=(
            P("gz", ("gy", "gx")),
            P("gz", ("gy", "gx")),
            P("gz", "gx"),
            P("gx", ("gy", "gz")),
        ),
        out_specs=(P("gz", ("gx", "gy")), P("gx", ("gy", "gz"))),
        check_vma=False,
    )
```

profile of v0, /device:TPU:2, one launch (start us, length us, event | category | flops | bytes accessed | tf_op | source)
XLA Modules:
  0.0 278.6 jit_solution(13331173982620140099)
XLA Ops:
  7.2 0.0 copy-start
  7.2 0.0 all-gather.3.cloned.1.call-start
  7.2 2.1 fusion.7
  9.3 0.0 all-gather.3.cloned.1.call-update
  9.4 0.0 all-gather.5.cloned.1.call-start
  9.4 0.7 all-gather.5.cloned.1.call-update
  10.1 51.4 %all-gather.3.cloned.1.call-done = bf16[384,3072]{1,0:T(8,128)(2,1)} async-done(((bf16[384,384]{1,0:T(8,128)(2,1)}), bf16[384,3072]{1,0:T(8,128)(2,1)}) %all-gather.3.cloned.1.call-update) | async-done | bytes 2359312 | tf_op jit(solution)/shard_map/all_gather | solution.py:36
  61.5 0.0 copy-done
  61.5 6.5 %convolution_convert_fusion = bf16[3072,768]{1,0:T(8,128)(2,1)} fusion(bf16[384,3072]{1,0:T(8,128)(2,1)} %all-gather.3.cloned.1.call-done, bf16[384,768]{1,0:T(8,128)(2,1)S(1)} %copy-done), kind=kOutput, calls=%fused_computation | convolution fusion | flops 1814298624 | bytes 7667712 | tf_op jit(solution)/shard_map/dot_general | solution.py:24
  68.0 0.0 copy-start.1
  68.0 6.7 %all-to-all-start = ((bf16[768,8,384]{0,2,1:T(8,128)(2,1)}), bf16[768,8,384]{0,2,1:T(8,128)(2,1)}, u32[]{:S(2)}, u32[]{:S(2)}) async-start(bf16[768,8,384]{0,2,1:T(8,128)(2,1)} %bitcast.7), calls=%async_computation.1 | async-start | bytes 9437184 | tf_op jit(solution)/shard_map/all_to_all | solution.py:42
  74.7 0.0 reduce-scatter.2.cloned.1.call-start
  74.8 140.1 %all-gather.5.cloned.1.call-done = bf16[768,3072]{1,0:T(8,128)(2,1)} async-done(((bf16[768,384]{1,0:T(8,128)(2,1)}), bf16[768,3072]{1,0:T(8,128)(2,1)}) %all-gather.5.cloned.1.call-update) | async-done | bytes 4718608 | tf_op jit(solution)/shard_map/all_gather | solution.py:35
  214.9 0.0 copy-done.1
  214.9 6.0 %fusion.8 = f32[384,768]{0,1:T(8,128)} fusion(bf16[384,3072]{1,0:T(8,128)(2,1)S(1)} %copy-done.1, bf16[768,3072]{1,0:T(8,128)(2,1)} %all-gather.5.cloned.1.call-done), kind=kOutput, calls=%fused_computation.13 | convolution fusion | flops 1811939328 | bytes 8257536 | tf_op jit(solution)/shard_map/dot_general | solution.py:18
  220.8 0.0 reduce-scatter.2.cloned.1.call-update
  220.9 45.3 %reduce-scatter.2.cloned.1.call-done = f32[384,96]{0,1:T(8,128)} async-done(((f32[384,768]{0,1:T(8,128)}), f32[384,96]{0,1:T(8,128)}) %reduce-scatter.2.cloned.1.call-update) | async-done | bytes 147472 | tf_op jit(solution)/shard_map/reduce_scatter | solution.py:44
  266.2 1.6 convert_element_type.23
  267.7 0.0 all-to-all-done
  267.7 3.3 %reduce_sum.12 = bf16[768,384]{0,1:T(8,128)(2,1)S(1)} reduce(bf16[768,8,384]{0,2,1:T(8,128)(2,1)} %all-to-all-done, bf16[]{:T(256)} %constant.12.clone.1), dimensions={1}, to_apply=%region_1.0 | reduce | flops 2064384 | bytes 5308418 | tf_op jit(solution)/shard_map/reduce_sum | solution.py:43
  271.0 1.1 copy.6
Async XLA Ops:
  7.2 54.3 %copy-start = (bf16[384,768]{1,0:T(8,128)(2,1)S(1)}, bf16[384,768]{1,0:T(8,128)(2,1)}, u32[]{:S(2)}) copy-start(bf16[384,768]{1,0:T(8,128)(2,1)} %param.6) | copy-start | bytes 1769476
  7.2 54.3 %all-gather.3.cloned.1.call-start = ((), (), s32[]{:S(2)}) async-start(), calls=%async_computation.2 | async-start | bytes 2654208 | tf_op jit(solution)/shard_map/all_gather | solution.py:36
  9.4 205.5 %all-gather.5.cloned.1.call-start = ((), (), s32[]{:S(2)}) async-start(), calls=%async_computation.3 | async-start | bytes 5308416 | tf_op jit(solution)/shard_map/all_gather | solution.py:35
  68.0 146.9 %copy-start.1 = (bf16[384,3072]{1,0:T(8,128)(2,1)S(1)}, bf16[384,3072]{1,0:T(8,128)(2,1)}, u32[]{:S(2)}) copy-start(bf16[384,3072]{1,0:T(8,128)(2,1)} %all-gather.3.cloned.1.call-done) | copy-start | bytes 7077892
  68.0 199.8 %all-to-all-start = ((bf16[768,8,384]{0,2,1:T(8,128)(2,1)}), bf16[768,8,384]{0,2,1:T(8,128)(2,1)}, u32[]{:S(2)}, u32[]{:S(2)}) async-start(bf16[768,8,384]{0,2,1:T(8,128)(2,1)} %bitcast.7), calls=%async_computation.1 | async-start | bytes 9437184 | tf_op jit(solution)/shard_map/all_to_all | solution.py:42
  74.7 191.5 %reduce-scatter.2.cloned.1.call-start = ((), (), s32[]{:S(2)}) async-start(), calls=%async_computation.4 | async-start | bytes 1327104 | tf_op jit(solution)/shard_map/reduce_scatter | solution.py:44
Sparse Core Ops, SparseCore 0:
  10.7 50.7 all-gather.2
  63.6 151.1 all-gather.4
  221.0 45.1 reduce-scatter.1
where the time goes:
time: 279 us
  waiting for transfers between devices  238 us (85%)
  between operations  13.8 us (5%)
  matrix products  12.5 us (4%)
  other arithmetic  6.94 us (2%)
  starting transfers between devices  6.86 us (2%)
    all_gather x1, waiting for transfers between devices, shards(): whole_weight = lax.all_gather(weight, 'gz', axis=1, tiled=True)  140 us
    all_gather x1, waiting for transfers between devices, shards(): piece = lax.all_gather(grad_hidden, 'gx', axis=1, tiled=True)  51.4 us
    reduce_scatter x1, waiting for transfers between devices, shards(): lax.psum_scatter(acc_inputs, 'gy', scatter_dimension=1, tiled=True)  45.3 us
    all_to_all x1, starting transfers between devices, shards(): lax.all_to_all(stacked, 'gz', split_axis=1, concat_axis=1, tiled=True)  6.74 us
    dot_general x1, matrix products, contract_first(): lax.dot_general(left, right, (((0,), (0,)), ((), ())), preferred_element_...  6.49 us
    dot_general x1, matrix products, contract_last(): lax.dot_general(left, right, (((1,), (1,)), ((), ())), preferred_element_...  5.98 us
  transfers between devices with their start and end apart: 4, of which 3 were waited for; matrix products, arithmetic and copies ran while one was open for 5% of the time, Pallas kernels for 0%

commit v1 on v0

v1 whole, which is shorter than its diff:
```python
import functools

import jax
import jax.numpy as jnp
from jax import lax
from jax.experimental import pallas as pl
from jax.experimental.pallas import tpu as pltpu
from jax.sharding import PartitionSpec as P

MESH = pl.DeviceIdType.MESH
root_half = 0.7071067811865476
inv_root_tau = 0.3989422804014327

TOK, FEAT, HID = 384, 768, 384
NY, NZ, NX = 8, 4, 4
SLICE = FEAT // NY
HALF = SLICE // 2
ORDER = (0, 1, 3, 2)


def gelu_grad(grad_act, pre_act):
    value = pre_act.astype(jnp.float32)
    cdf = 0.5 * (1.0 + lax.erf(value * root_half))
    pdf = jnp.exp(-0.5 * value * value) * inv_root_tau
    return (grad_act.astype(jnp.float32) * (cdf + value * pdf)).astype(jnp.bfloat16)


def mod(value, size):
    return lax.rem(value + size, size)


def kernel(
    ga, pa, inp, w, git, gw,
    gh, ghs, inputs_t, total, pair_out, pair_in, up_out, down_out, up_in, down_in, z_out, z_in, acc,
    send_sem, gh_sem, col_sem, ring_sem, core_sem, pair_sem, up_sem, down_sem, z_sem,
):
    gx, y, gz = (lax.axis_index(name) for name in ("gx", "gy", "gz"))
    zl, x = lax.div(gx, NX), lax.rem(gx, NX)
    zh, c = lax.div(gz, 2), lax.rem(gz, 2)

    def device(x=x, zl=zl, y=y, zh=zh, c=c):
        return (zl * NX + x, y, zh * 2 + c)

    other_core = device(c=1 - c)
    above, below = device(y=mod(y + 1, NY)), device(y=mod(y - 1, NY))
    at_z = [device(zh=mod(zh + k, NZ)) for k in range(NZ)]

    home_zh, home_c = lax.div(x, 2) + 2 * zl, lax.rem(x, 2)
    at_home = jnp.logical_and(home_zh == zh, home_c == c)
    root_x = 2 * lax.rem(zh, 2) + c
    step_x = 2 * c - 1
    role = lax.rem((x - root_x) * step_x + 2 * NX, NX)
    is_root, is_relay = role == 0, role == 1
    onward, backward = device(x=mod(x + step_x, NX)), device(x=mod(x - step_x, NX))

    barrier = pltpu.get_barrier_semaphore()

    def hello(dev):
        pl.semaphore_signal(barrier, inc=1, device_id=dev, device_id_type=MESH)

    for dev in (other_core, above, below, onward, backward, at_z[1], at_z[2], at_z[3]):
        hello(dev)
    src_zl = lax.div(zh, 2)
    for k in range(NZ):
        for core in range(2):
            here = jnp.logical_and(zl == src_zl, jnp.logical_and(zh == k, c == core))

            @pl.when(jnp.logical_and(is_root, jnp.logical_not(here)))
            def _():
                hello(device(zl=src_zl, zh=k, c=core))
    pl.semaphore_wait(barrier, 10 - at_home.astype(jnp.int32))

    sends = []

    def remote(src, dst, recv, dev, cond=None):
        copy = pltpu.make_async_remote_copy(
            src_ref=src, dst_ref=dst, send_sem=send_sem.at[len(sends)], recv_sem=recv,
            device_id=dev, device_id_type=MESH,
        )
        sends.append((copy, cond))
        if cond is None:
            copy.start()
        else:
            pl.when(cond)(copy.start)

    def arrived(dst, recv):
        pltpu.make_async_remote_copy(
            src_ref=dst, dst_ref=dst, send_sem=send_sem.at[0], recv_sem=recv,
            device_id=other_core, device_id_type=MESH,
        ).wait_recv()

    for r in range(0, TOK, 64):
        gh[r : r + 64, :] = gelu_grad(ga[r : r + 64, :], pa[r : r + 64, :])
    far = mod(zh - home_zh, NZ)
    for zl_to in range(2):
        local = jnp.logical_and(at_home, zl == zl_to)
        remote(
            gh, ghs.at[far, c], gh_sem.at[far * 2 + c],
            device(zl=zl_to, zh=home_zh, c=home_c), jnp.logical_not(local),
        )

        @pl.when(local)
        def _():
            pltpu.make_async_copy(gh, ghs.at[0, c], gh_sem.at[c]).start()

    inputs_t[c, 0] = inp[...].astype(jnp.float32).T.astype(jnp.bfloat16).reshape(NY, SLICE, TOK)
    for k in range(1, NZ):
        remote(inputs_t.at[c, 0, y], inputs_t.at[c, k, y], col_sem.at[k - 1], at_z[NZ - k])
    remote(inputs_t.at[c, 0], inputs_t.at[c, 0], core_sem.at[0], other_core)

    def piece(who, rows=None):
        who = mod(who, NY)
        if rows is None:
            return inputs_t.at[c, pl.ds(1, NZ - 1), who]
        return inputs_t.at[c, pl.ds(1, NZ - 1), who, pl.ds(rows, HALF)]

    def inputs_ring(step):
        if step == 0:
            for k in range(1, NZ):
                arrived(inputs_t.at[c, k, y], col_sem.at[k - 1])
        elif step < 4:
            arrived(piece(y - step), ring_sem.at[step - 1])
            arrived(piece(y + step), ring_sem.at[4 + step - 1])
        else:
            arrived(piece(y - 4, 0), ring_sem.at[3])
            arrived(piece(y + 4, HALF), ring_sem.at[7])
            rest = inputs_t.at[c, pl.ds(1, NZ - 1)]
            remote(rest, rest, core_sem.at[1], other_core)
            return
        lo, hi = (0, HALF) if step == 3 else (None, None)
        remote(piece(y - step, lo), piece(y - step, lo), ring_sem.at[step], above)
        remote(piece(y + step, hi), piece(y + step, hi), ring_sem.at[4 + step], below)

    def gather(k):
        for core in range(2):
            block, sem = ghs.at[k, core], gh_sem.at[2 * k + core]
            arrived(block, sem)
            remote(block, block, sem, onward, jnp.logical_or(is_root, is_relay))
            remote(block, block, sem, backward, is_root)

    def product(k, core):
        return lax.dot_general(
            w[...], ghs[k, core], (((1,), (1,)), ((), ())), preferred_element_type=jnp.float32
        ).reshape(NY, SLICE, TOK)

    def compute(k):
        pair_out[k] = product(k, 1 - c).astype(jnp.bfloat16)
        remote(pair_out.at[k], pair_in.at[k], pair_sem.at[k], other_core)
        total[k] = product(k, c)

    def add_pair(k):
        arrived(pair_in.at[k], pair_sem.at[k])
        total[k] = total[k] + pair_in[k].astype(jnp.float32)

    def reduce(k, step):
        up_to, down_to = mod(y + 5 - step, NY), mod(y - 5 + step, NY)
        up_dst, down_dst = up_in.at[k, step - 1], down_in.at[k, step - 1]
        up_src, down_src = up_out.at[k, step - 1], down_out.at[k, step - 1]
        lo, hi = pl.ds(0, HALF), pl.ds(HALF, HALF)
        if step == 1:
            up_out[k, 0, lo] = total[k, up_to, lo].astype(jnp.bfloat16)
            down_out[k, 0, hi] = total[k, down_to, hi].astype(jnp.bfloat16)
            up_src, up_dst = up_src.at[lo], up_dst.at[lo]
            down_src, down_dst = down_src.at[hi], down_dst.at[hi]
        elif step == 2:
            arrived(up_in.at[k, 0, lo], up_sem.at[4 * k])
            up_out[k, 1, lo] = (total[k, up_to, lo] + up_in[k, 0, lo].astype(jnp.float32)).astype(jnp.bfloat16)
            up_out[k, 1, hi] = total[k, up_to, hi].astype(jnp.bfloat16)
            arrived(down_in.at[k, 0, hi], down_sem.at[4 * k])
            down_out[k, 1, hi] = (total[k, down_to, hi] + down_in[k, 0, hi].astype(jnp.float32)).astype(jnp.bfloat16)
            down_out[k, 1, lo] = total[k, down_to, lo].astype(jnp.bfloat16)
        else:
            arrived(up_in.at[k, step - 2], up_sem.at[4 * k + step - 2])
            up_out[k, step - 1] = (total[k, up_to] + up_in[k, step - 2].astype(jnp.float32)).astype(jnp.bfloat16)
            arrived(down_in.at[k, step - 2], down_sem.at[4 * k + step - 2])
            down_out[k, step - 1] = (total[k, down_to] + down_in[k, step - 2].astype(jnp.float32)).astype(jnp.bfloat16)
        remote(up_src, up_dst, up_sem.at[4 * k + step - 1], above)
        remote(down_src, down_dst, down_sem.at[4 * k + step - 1], below)

    def finish(k):
        arrived(up_in.at[k, 3], up_sem.at[4 * k + 3])
        arrived(down_in.at[k, 3], down_sem.at[4 * k + 3])
        whole = total[k, y] + up_in[k, 3].astype(jnp.float32) + down_in[k, 3].astype(jnp.float32)
        if k == 0:
            total[0, y] = whole
        else:
            z_out[k - 1] = whole.astype(jnp.bfloat16)
            remote(z_out.at[k - 1], z_in.at[k - 1], z_sem.at[k - 1], at_z[k])

    def weight_grad(k):
        for core in range(2):
            term = lax.dot_general(
                inputs_t[core, k].reshape(FEAT, TOK), ghs[k, core], (((1,), (0,)), ((), ())),
                preferred_element_type=jnp.float32,
            )
            if k == 0 and core == 0:
                acc[...] = term
            else:
                acc[...] += term

    a, b, d, e = ORDER
    gather(a)
    inputs_ring(0)
    compute(a)
    add_pair(a)
    reduce(a, 1)
    inputs_ring(1)
    gather(b)
    compute(b)
    reduce(a, 2)
    add_pair(b)
    reduce(b, 1)
    reduce(a, 3)
    inputs_ring(2)
    gather(d)
    reduce(a, 4)
    reduce(b, 2)
    compute(d)
    add_pair(d)
    reduce(d, 1)
    finish(a)
    reduce(b, 3)
    inputs_ring(3)
    gather(e)
    reduce(b, 4)
    reduce(d, 2)
    compute(e)
    add_pair(e)
    reduce(e, 1)
    finish(b)
    reduce(d, 3)
    inputs_ring(4)
    reduce(e, 2)
    reduce(d, 4)
    arrived(inputs_t.at[1 - c, 0], core_sem.at[0])
    weight_grad(0)
    reduce(e, 3)
    finish(d)
    arrived(inputs_t.at[1 - c, pl.ds(1, NZ - 1)], core_sem.at[1])
    weight_grad(1)
    reduce(e, 4)
    weight_grad(2)
    weight_grad(3)
    gw[...] = acc[...].astype(jnp.bfloat16)
    finish(e)
    for k in range(NZ - 1):
        arrived(z_in.at[k], z_sem.at[k])
    out = total[0, y]
    for k in range(NZ - 1):
        out = out + z_in[k].astype(jnp.float32)
    git[...] = out.astype(jnp.bfloat16)

    for copy, cond in sends:
        if cond is None:
            copy.wait_send()
        else:
            pl.when(cond)(copy.wait_send)


N_SENDS = 2 + 4 + 8 + 1 + 16 + 4 + 32 + 3


def shards(grad_act, pre_act, inputs, weight):
    vmem = pl.BlockSpec(memory_space=pltpu.VMEM)
    bf16, f32 = jnp.bfloat16, jnp.float32
    dma = pltpu.SemaphoreType.DMA
    git, gw = pl.pallas_call(
        kernel,
        out_shape=(
            jax.ShapeDtypeStruct((SLICE, TOK), bf16),
            jax.ShapeDtypeStruct((FEAT, HID), bf16),
        ),
        in_specs=[vmem] * 4,
        out_specs=(vmem, vmem),
        scratch_shapes=[
            pltpu.VMEM((TOK, HID), bf16),
            pltpu.VMEM((NZ, 2, TOK, HID), bf16),
            pltpu.VMEM((2, NZ, NY, SLICE, TOK), bf16),
            pltpu.VMEM((NZ, NY, SLICE, TOK), f32),
            pltpu.VMEM((NZ, NY, SLICE, TOK), bf16),
            pltpu.VMEM((NZ, NY, SLICE, TOK), bf16),
            pltpu.VMEM((NZ, 4, SLICE, TOK), bf16),
            pltpu.VMEM((NZ, 4, SLICE, TOK), bf16),
            pltpu.VMEM((NZ, 4, SLICE, TOK), bf16),
            pltpu.VMEM((NZ, 4, SLICE, TOK), bf16),
            pltpu.VMEM((NZ - 1, SLICE, TOK), bf16),
            pltpu.VMEM((NZ - 1, SLICE, TOK), bf16),
            pltpu.VMEM((FEAT, HID), f32),
            dma((N_SENDS,)),
            dma((2 * NZ,)),
            dma((NZ - 1,)),
            dma((8,)),
            dma((2,)),
            dma((NZ,)),
            dma((4 * NZ,)),
            dma((4 * NZ,)),
            dma((NZ - 1,)),
        ],
        compiler_params=pltpu.CompilerParams(
            collective_id=0, has_side_effects=True, vmem_limit_bytes=48 * 2**20
        ),
    )(grad_act, pre_act, inputs, weight)
    return git.T, gw


def solution(mesh):
    return jax.shard_map(
        shards,
        mesh=mesh,
        in_specs=(
            P("gz", ("gy", "gx")),
            P("gz", ("gy", "gx")),
            P("gz", "gx"),
            P("gx", ("gy", "gz")),
        ),
        out_specs=(P("gz", ("gx", "gy")), P("gx", ("gy", "gz"))),
        check_vma=False,
    )
```

time: 279 us -> 116 us (0.42)
  the two profiles are of different devices: /device:TPU:2 before, /device:TPU:68 now
where the time goes in v1:
time: 116 us; the launch traced here: 115 us
  Pallas kernels  109 us (94%)
  local copies, waits for them, and re-layouts  5.49 us (5%)
    pallas_call x1, Pallas kernels, shards(): pl.pallas_call(kernel, out_shape=(jax.ShapeDtypeStruct((SLICE, TOK), bf16...  109 us
    unnamed x10, local copies, waits for them, and re-layouts  5.49 us

profile of v1, /device:TPU:68, one launch (start us, length us, event | category | flops | bytes accessed | tf_op | source)
XLA Modules:
  0.0 115.5 jit_solution(15363494565554926018)
XLA Ops:
  0.6 0.0 copy-start
  0.6 1.1 copy-done
  1.7 0.0 copy-start.1
  1.7 1.1 copy-done.1
  2.8 0.0 copy-start.2
  2.8 1.0 copy-done.2
  3.7 0.0 copy-start.3
  3.7 1.0 copy-done.3
  4.7 109.4 %shard_map.59 = (bf16[96,384]{1,0:T(8,128)(2,1)S(1)}, bf16[768,384]{1,0:T(8,128)(2,1)S(1)}) custom-call(bf16[384,384]{1,0:T(8,128)(2,1)S(1)} %copy-done.2, bf16[384,384]{1,0:T(8,128)(2,1)S(1)} %copy-done.3, bf16[384,768]{1,0:T(8,128)(2,1)S(1)} %copy-done, bf16[768,384]{1,0:T(8,128)(2,1)S(1)} %copy-done.1), custom_call_target="tpu_custom_call" | custom-call | tf_op jit(solution)/shard_map/pallas_call | solution.py:267
  114.0 0.6 copy.8
  114.7 0.8 copy.9
Async XLA Ops:
  0.6 1.1 copy-start
  1.7 1.1 copy-start.1
  2.8 1.0 copy-start.2
  3.7 1.0 copy-start.3

commit v2 on v1

v2 whole, which is shorter than its diff:
```python
import functools

import jax
import jax.numpy as jnp
from jax import lax
from jax.experimental import pallas as pl
from jax.experimental.pallas import tpu as pltpu
from jax.sharding import PartitionSpec as P

MESH = pl.DeviceIdType.MESH
root_half = 0.7071067811865476
inv_root_tau = 0.3989422804014327

TOK, FEAT, HID = 384, 768, 384
NY, NZ, NX = 8, 4, 4
SLICE = FEAT // NY
HALF = SLICE // 2
PARTS = 2
ROWS = TOK // PARTS
ONE_ROW = (1,)


def gelu_grad(grad_act, pre_act):
    value = pre_act.astype(jnp.float32)
    cdf = 0.5 * (1.0 + lax.erf(value * root_half))
    pdf = jnp.exp(-0.5 * value * value) * inv_root_tau
    return (grad_act.astype(jnp.float32) * (cdf + value * pdf)).astype(jnp.bfloat16)


def mod(value, size):
    return lax.rem(value + size, size)


def kernel(
    ga_any, pa_any, inp_any, w_any, git, gw,
    ga, pa, inp, w, gh, ghs, inputs_t, total, pair_out, pair_in, up_out, down_out, up_in, down_in, z_out, z_in, acc,
    load_sem, send_sem, gh_sem, col_sem, ring_sem, core_sem, pair_sem, up_sem, down_sem, z_sem,
):
    loads = [
        pltpu.make_async_copy(src, dst, load_sem.at[i])
        for i, (src, dst) in enumerate(((pa_any, pa), (ga_any, ga), (inp_any, inp), (w_any, w)))
    ]
    for copy in loads:
        copy.start()

    gx, y, gz = (lax.axis_index(name) for name in ("gx", "gy", "gz"))
    zl, x = lax.div(gx, NX), lax.rem(gx, NX)
    zh, c = lax.div(gz, 2), lax.rem(gz, 2)

    def device(x=x, zl=zl, y=y, zh=zh, c=c):
        return (zl * NX + x, y, zh * 2 + c)

    other_core = device(c=1 - c)
    above, below = device(y=mod(y + 1, NY)), device(y=mod(y - 1, NY))
    at_z = [device(zh=mod(zh + k, NZ)) for k in range(NZ)]

    home_zh, home_c = lax.div(x, 2) + 2 * zl, lax.rem(x, 2)
    at_home = jnp.logical_and(home_zh == zh, home_c == c)
    root_x = 2 * lax.rem(zh, 2) + c
    step_x = 2 * c - 1
    role = lax.rem((x - root_x) * step_x + 2 * NX, NX)
    is_root, is_relay = role == 0, role == 1
    onward, backward = device(x=mod(x + step_x, NX)), device(x=mod(x - step_x, NX))

    barrier = pltpu.get_barrier_semaphore()

    def hello(dev):
        pl.semaphore_signal(barrier, inc=1, device_id=dev, device_id_type=MESH)

    other_zl = device(zl=1 - zl)
    for dev in (other_core, above, below, onward, backward, other_zl, at_z[1], at_z[2], at_z[3]):
        hello(dev)

    def first_zl(k, owner_zl):
        return (owner_zl, 1, 1 - owner_zl, 0)[k]

    src_zl = lax.div(zh, 2)
    for k in range(NZ):
        for core in range(2):
            expected = jnp.logical_and(is_root, first_zl(k, src_zl) == zl)
            if k == 0:
                expected = jnp.logical_and(expected, c != core)

            @pl.when(expected)
            def _():
                hello(device(zl=src_zl, zh=mod(zh + k, NZ), c=core))

    sends = []

    def remote(src, dst, recv, dev, cond=None):
        copy = pltpu.make_async_remote_copy(
            src_ref=src, dst_ref=dst, send_sem=send_sem.at[len(sends)], recv_sem=recv,
            device_id=dev, device_id_type=MESH,
        )
        sends.append((copy, cond))
        if cond is None:
            copy.start()
        else:
            pl.when(cond)(copy.start)

    def arrived(dst, recv):
        pltpu.make_async_remote_copy(
            src_ref=dst, dst_ref=dst, send_sem=send_sem.at[0], recv_sem=recv,
            device_id=other_core, device_id_type=MESH,
        ).wait_recv()

    loads[0].wait()
    loads[1].wait()
    for r in range(0, TOK, 64):
        gh[r : r + 64, :] = gelu_grad(ga[r : r + 64, :], pa[r : r + 64, :])
    loads[2].wait()
    inputs_t[c, 0] = inp[...].astype(jnp.float32).T.astype(jnp.bfloat16).reshape(NY, SLICE, TOK)
    pl.semaphore_wait(barrier, 10 - at_home.astype(jnp.int32))

    def send_inputs():
        for k in range(1, NZ):
            remote(inputs_t.at[c, 0, y], inputs_t.at[c, k, y], col_sem.at[k - 1], at_z[NZ - k])

    far = mod(zh - home_zh, NZ)

    def hidden_part(k, core, part):
        return ghs.at[k, core, pl.ds(part * ROWS, ROWS)], gh_sem.at[(2 * k + core) * PARTS + part]

    def send_hidden(turn):
        first = jnp.where(far == 0, zl, jnp.where(far == 1, 1, jnp.where(far == 2, 1 - zl, 0)))
        for part in range(PARTS):
            block, sem = hidden_part(far, c, part)
            remote(
                gh.at[pl.ds(part * ROWS, ROWS)], block, sem,
                device(zl=first, zh=home_zh, c=home_c), jnp.logical_and(turn, jnp.logical_not(at_home)),
            )

    def keep_hidden():
        @pl.when(at_home)
        def _():
            for part in range(PARTS):
                block, sem = hidden_part(0, c, part)
                pltpu.make_async_copy(gh.at[pl.ds(part * ROWS, ROWS)], block, sem).start()

    def share_inputs():
        remote(inputs_t.at[c, 0], inputs_t.at[c, 0], core_sem.at[0], other_core)

    def piece(k, who, rows=None):
        block = inputs_t.at[c, k, mod(who, NY)]
        return block if rows is None else block.at[pl.ds(rows, HALF)]

    def inputs_ring(step):
        for k in range(1, NZ):
            up, down = 8 * (k - 1), 8 * (k - 1) + 4
            if step == 0:
                arrived(piece(k, y), col_sem.at[k - 1])
            elif step < 4:
                arrived(piece(k, y - step), ring_sem.at[up + step - 1])
                arrived(piece(k, y + step), ring_sem.at[down + step - 1])
            else:
                arrived(piece(k, y - 4, 0), ring_sem.at[up + 3])
                arrived(piece(k, y + 4, HALF), ring_sem.at[down + 3])
                remote(inputs_t.at[c, k], inputs_t.at[c, k], core_sem.at[k], other_core)
                continue
            lo, hi = (0, HALF) if step == 3 else (None, None)
            remote(piece(k, y - step, lo), piece(k, y - step, lo), ring_sem.at[up + step], above)
            remote(piece(k, y + step, hi), piece(k, y + step, hi), ring_sem.at[down + step], below)

    home_row = zl == src_zl
    near = 3 - 2 * zl
    groups = [jnp.where(home_row, *pair) for pair in ((0, near), (near, 0), (4 - near, 2), (2, 4 - near))]
    first_here = (True, home_row, jnp.logical_not(home_row), False)

    def both(*conds):
        return functools.reduce(jnp.logical_and, conds)

    def gather(n, who):
        k, first = groups[n], first_here[n]
        for part in range(PARTS):
            for core in range(2):
                block, sem = hidden_part(k, core, part)
                one_row = core in ONE_ROW

                @pl.when(who)
                def _():
                    arrived(block, sem)

                go = who
                if one_row:
                    go = None if first is False else both(who, first)
                if go is not None and (who is is_root or who is is_relay):
                    remote(block, block, sem, onward, go)
                if go is not None and who is is_root:
                    remote(block, block, sem, backward, go)
                if first is not False and (who is is_root or one_row):
                    remote(block, block, sem, other_zl, both(who, first))

    is_leaf = role >= 2

    def product(k, core):
        return lax.dot_general(
            w[...], ghs[k, core], (((1,), (1,)), ((), ())), preferred_element_type=jnp.float32
        ).reshape(NY, SLICE, TOK)

    def compute(n):
        k = groups[n]
        pair_out[k] = product(k, 1 - c).astype(jnp.bfloat16)
        remote(pair_out.at[k], pair_in.at[k], pair_sem.at[k], other_core)
        total[k] = product(k, c)

    def add_pair(n):
        k = groups[n]
        arrived(pair_in.at[k], pair_sem.at[k])
        total[k] = total[k] + pair_in[k].astype(jnp.float32)

    def reduce(n, step):
        k = groups[n]
        up_to, down_to = mod(y + 5 - step, NY), mod(y - 5 + step, NY)
        up_dst, down_dst = up_in.at[k, step - 1], down_in.at[k, step - 1]
        up_src, down_src = up_out.at[k, step - 1], down_out.at[k, step - 1]
        lo, hi = pl.ds(0, HALF), pl.ds(HALF, HALF)
        if step == 1:
            up_out[k, 0, lo] = total[k, up_to, lo].astype(jnp.bfloat16)
            down_out[k, 0, hi] = total[k, down_to, hi].astype(jnp.bfloat16)
            up_src, up_dst = up_src.at[lo], up_dst.at[lo]
            down_src, down_dst = down_src.at[hi], down_dst.at[hi]
        elif step == 2:
            arrived(up_in.at[k, 0, lo], up_sem.at[4 * k])
            up_out[k, 1, lo] = (total[k, up_to, lo] + up_in[k, 0, lo].astype(jnp.float32)).astype(jnp.bfloat16)
            up_out[k, 1, hi] = total[k, up_to, hi].astype(jnp.bfloat16)
            arrived(down_in.at[k, 0, hi], down_sem.at[4 * k])
            down_out[k, 1, hi] = (total[k, down_to, hi] + down_in[k, 0, hi].astype(jnp.float32)).astype(jnp.bfloat16)
            down_out[k, 1, lo] = total[k, down_to, lo].astype(jnp.bfloat16)
        else:
            arrived(up_in.at[k, step - 2], up_sem.at[4 * k + step - 2])
            up_out[k, step - 1] = (total[k, up_to] + up_in[k, step - 2].astype(jnp.float32)).astype(jnp.bfloat16)
            arrived(down_in.at[k, step - 2], down_sem.at[4 * k + step - 2])
            down_out[k, step - 1] = (total[k, down_to] + down_in[k, step - 2].astype(jnp.float32)).astype(jnp.bfloat16)
        remote(up_src, up_dst, up_sem.at[4 * k + step - 1], above)
        remote(down_src, down_dst, down_sem.at[4 * k + step - 1], below)

    def finish(n):
        k = groups[n]
        arrived(up_in.at[k, 3], up_sem.at[4 * k + 3])
        arrived(down_in.at[k, 3], down_sem.at[4 * k + 3])
        whole = total[k, y] + up_in[k, 3].astype(jnp.float32) + down_in[k, 3].astype(jnp.float32)
        total[k, y] = whole
        z_out[k] = whole.astype(jnp.bfloat16)
        remote(z_out.at[k], z_in.at[k], z_sem.at[k], device(zh=mod(zh + k, NZ)), k != 0)

    def weight_grad(k):
        arrived(inputs_t.at[1 - c, k], core_sem.at[k])
        for core in range(2):
            term = lax.dot_general(
                inputs_t[core, k].reshape(FEAT, TOK), ghs[k, core], (((1,), (0,)), ((), ())),
                preferred_element_type=jnp.float32,
            )
            if k == 0 and core == 0:
                acc[...] = term
            else:
                acc[...] += term

    def write_weight_grad():
        gw[...] = acc[...].astype(jnp.bfloat16)

    def write_inputs_grad():
        out = total[0, y]
        for k in range(1, NZ):
            arrived(z_in.at[k], z_sem.at[k])
            out = out + z_in[k].astype(jnp.float32)
        git[...] = out.astype(jnp.bfloat16)

    loads[3].wait()
    root, relay, leaf, role2, role3 = is_root, is_relay, is_leaf, role == 2, role == 3
    schedule = (
        (send_inputs,), (keep_hidden,), (send_hidden, far != 2), (share_inputs,), (gather, 0, root),
        (inputs_ring, 0), (gather, 1, root), (send_hidden, both(far == 2, root)), (gather, 0, role3), (send_hidden, both(far == 2, role3)),
        (gather, 0, relay), (inputs_ring, 1), (gather, 0, role2),
        (compute, 0), (gather, 2, root), (gather, 1, relay), (add_pair, 0), (reduce, 0, 1), (inputs_ring, 2),
        (gather, 3, root), (gather, 1, leaf), (compute, 1), (gather, 2, relay), (reduce, 0, 2), (inputs_ring, 3),
        (add_pair, 1), (reduce, 1, 1), (reduce, 0, 3), (gather, 2, leaf), (compute, 2), (inputs_ring, 4),
        (gather, 3, relay), (reduce, 1, 2), (reduce, 0, 4), (add_pair, 2), (reduce, 2, 1), (reduce, 1, 3),
        (finish, 0), (gather, 3, leaf), (compute, 3), (reduce, 2, 2), (reduce, 1, 4), (add_pair, 3), (reduce, 3, 1),
        (reduce, 2, 3), (finish, 1), (weight_grad, 0), (reduce, 3, 2), (reduce, 2, 4), (weight_grad, 1),
        (reduce, 3, 3), (finish, 2), (weight_grad, 2), (reduce, 3, 4), (weight_grad, 3), (write_weight_grad,),
        (finish, 3), (write_inputs_grad,),
    )
    for step, *args in schedule:
        step(*args)

    for copy, cond in sends:
        if cond is None:
            copy.wait_send()
        else:
            pl.when(cond)(copy.wait_send)


N_SENDS = 192


def shards(grad_act, pre_act, inputs, weight):
    vmem = pl.BlockSpec(memory_space=pltpu.VMEM)
    bf16, f32 = jnp.bfloat16, jnp.float32
    dma = pltpu.SemaphoreType.DMA
    git, gw = pl.pallas_call(
        kernel,
        out_shape=(
            jax.ShapeDtypeStruct((SLICE, TOK), bf16),
            jax.ShapeDtypeStruct((FEAT, HID), bf16),
        ),
        in_specs=[pl.BlockSpec(memory_space=pl.ANY)] * 4,
        out_specs=(vmem, vmem),
        scratch_shapes=[
            pltpu.VMEM((TOK, HID), bf16),
            pltpu.VMEM((TOK, HID), bf16),
            pltpu.VMEM((TOK, FEAT), bf16),
            pltpu.VMEM((FEAT, HID), bf16),
            pltpu.VMEM((TOK, HID), bf16),
            pltpu.VMEM((NZ, 2, TOK, HID), bf16),
            pltpu.VMEM((2, NZ, NY, SLICE, TOK), bf16),
            pltpu.VMEM((NZ, NY, SLICE, TOK), f32),
            pltpu.VMEM((NZ, NY, SLICE, TOK), bf16),
            pltpu.VMEM((NZ, NY, SLICE, TOK), bf16),
            pltpu.VMEM((NZ, 4, SLICE, TOK), bf16),
            pltpu.VMEM((NZ, 4, SLICE, TOK), bf16),
            pltpu.VMEM((NZ, 4, SLICE, TOK), bf16),
            pltpu.VMEM((NZ, 4, SLICE, TOK), bf16),
            pltpu.VMEM((NZ, SLICE, TOK), bf16),
            pltpu.VMEM((NZ, SLICE, TOK), bf16),
            pltpu.VMEM((FEAT, HID), f32),
            dma((4,)),
            dma((N_SENDS,)),
            dma((2 * NZ * PARTS,)),
            dma((NZ - 1,)),
            dma((8 * (NZ - 1),)),
            dma((NZ,)),
            dma((NZ,)),
            dma((4 * NZ,)),
            dma((4 * NZ,)),
            dma((NZ,)),
        ],
        compiler_params=pltpu.CompilerParams(
            collective_id=0, has_side_effects=True, vmem_limit_bytes=60 * 2**20
        ),
    )(grad_act, pre_act, inputs, weight)
    return git.T, gw


def solution(mesh):
    return jax.shard_map(
        shards,
        mesh=mesh,
        in_specs=(
            P("gz", ("gy", "gx")),
            P("gz", ("gy", "gx")),
            P("gz", "gx"),
            P("gx", ("gy", "gz")),
        ),
        out_specs=(P("gz", ("gx", "gy")), P("gx", ("gy", "gz"))),
        check_vma=False,
    )
```

time: 116 us -> 93 us (0.80)
  the two profiles are of different devices: /device:TPU:68 before, /device:TPU:64 now
where the time goes in v2:
time: 93 us; the launch traced here: 92.7 us
  Pallas kernels  88.6 us (95%)
  local copies, waits for them, and re-layouts  3.46 us (4%)
    pallas_call x1, Pallas kernels, shards(): pl.pallas_call(kernel, out_shape=(jax.ShapeDtypeStruct((SLICE, TOK), bf16...  88.6 us
    unnamed x2, local copies, waits for them, and re-layouts  3.46 us

profile of v2, /device:TPU:64, one launch (start us, length us, event | category | flops | bytes accessed | tf_op | source)
XLA Modules:
  0.0 92.7 jit_solution(2840585771162575894)
XLA Ops:
  0.6 88.6 %shard_map.59 = (bf16[96,384]{1,0:T(8,128)(2,1)}, bf16[768,384]{1,0:T(8,128)(2,1)}) custom-call(bf16[384,384]{1,0:T(8,128)(2,1)} %ga_any.1, bf16[384,384]{1,0:T(8,128)(2,1)} %pa_any.1, bf16[384,768]{1,0:T(8,128)(2,1)} %inp_any.1, bf16[768,384]{1,0:T(8,128)(2,1)} %w_any.1), custom_call_target="tpu_custom_call" | custom-call | tf_op jit(solution)/shard_map/pallas_call | solution.py:300
  89.3 1.5 %copy.8 = bf16[384,96]{0,1:T(8,128)(2,1)} copy(bf16[384,96]{0,1:T(8,128)(2,1)} %bitcast.1) | data formatting | bytes 147456
  90.8 1.9 %copy.9 = bf16[768,384]{1,0:T(8,128)(2,1)} copy(bf16[768,384]{1,0:T(8,128)(2,1)} %get-tuple-element.9) | data formatting | bytes 1179648

commit v3 on v2

--- a/solution.py
+++ b/solution.py
@@ -15,7 +15,7 @@
 NY, NZ, NX = 8, 4, 4
 SLICE = FEAT // NY
 HALF = SLICE // 2
-PARTS = 2
+PARTS = 3
 ROWS = TOK // PARTS
 ONE_ROW = (1,)
 
@@ -85,6 +85,10 @@
             def _():
                 hello(device(zl=src_zl, zh=mod(zh + k, NZ), c=core))
 
+    @pl.when(jnp.logical_and(is_root, jnp.logical_and(zl != src_zl, c == 1)))
+    def _():
+        hello(device(zl=src_zl, c=0))
+
     sends = []
 
     def remote(src, dst, recv, dev, cond=None):
@@ -110,18 +114,22 @@
         gh[r : r + 64, :] = gelu_grad(ga[r : r + 64, :], pa[r : r + 64, :])
     loads[2].wait()
     inputs_t[c, 0] = inp[...].astype(jnp.float32).T.astype(jnp.bfloat16).reshape(NY, SLICE, TOK)
-    pl.semaphore_wait(barrier, 10 - at_home.astype(jnp.int32))
+    across = jnp.where(jnp.logical_and(home_zh == zh, c == 0), home_c, 0)
+    pl.semaphore_wait(barrier, 10 - at_home.astype(jnp.int32) + across)
 
     def send_inputs():
         for k in range(1, NZ):
             remote(inputs_t.at[c, 0, y], inputs_t.at[c, k, y], col_sem.at[k - 1], at_z[NZ - k])
 
+    def both(*conds):
+        return functools.reduce(jnp.logical_and, conds)
+
     far = mod(zh - home_zh, NZ)
 
     def hidden_part(k, core, part):
         return ghs.at[k, core, pl.ds(part * ROWS, ROWS)], gh_sem.at[(2 * k + core) * PARTS + part]
 
-    def send_hidden(turn):
+    def send_hidden(turn, direct=False):
         first = jnp.where(far == 0, zl, jnp.where(far == 1, 1, jnp.where(far == 2, 1 - zl, 0)))
         for part in range(PARTS):
             block, sem = hidden_part(far, c, part)
@@ -129,6 +137,11 @@
                 gh.at[pl.ds(part * ROWS, ROWS)], block, sem,
                 device(zl=first, zh=home_zh, c=home_c), jnp.logical_and(turn, jnp.logical_not(at_home)),
             )
+            if direct:
+                remote(
+                    gh.at[pl.ds(part * ROWS, ROWS)], block, sem,
+                    device(zl=1 - zl, zh=home_zh, c=home_c), both(far == 0, c == 0),
+                )
 
     def keep_hidden():
         @pl.when(at_home)
@@ -144,30 +157,26 @@
         block = inputs_t.at[c, k, mod(who, NY)]
         return block if rows is None else block.at[pl.ds(rows, HALF)]
 
-    def inputs_ring(step):
-        for k in range(1, NZ):
-            up, down = 8 * (k - 1), 8 * (k - 1) + 4
-            if step == 0:
-                arrived(piece(k, y), col_sem.at[k - 1])
-            elif step < 4:
-                arrived(piece(k, y - step), ring_sem.at[up + step - 1])
-                arrived(piece(k, y + step), ring_sem.at[down + step - 1])
-            else:
-                arrived(piece(k, y - 4, 0), ring_sem.at[up + 3])
-                arrived(piece(k, y + 4, HALF), ring_sem.at[down + 3])
-                remote(inputs_t.at[c, k], inputs_t.at[c, k], core_sem.at[k], other_core)
-                continue
-            lo, hi = (0, HALF) if step == 3 else (None, None)
-            remote(piece(k, y - step, lo), piece(k, y - step, lo), ring_sem.at[up + step], above)
-            remote(piece(k, y + step, hi), piece(k, y + step, hi), ring_sem.at[down + step], below)
+    def inputs_ring(step, k):
+        up, down = 8 * (k - 1), 8 * (k - 1) + 4
+        if step == 0:
+            arrived(piece(k, y), col_sem.at[k - 1])
+        elif step < 4:
+            arrived(piece(k, y - step), ring_sem.at[up + step - 1])
+            arrived(piece(k, y + step), ring_sem.at[down + step - 1])
+        else:
+            arrived(piece(k, y - 4, 0), ring_sem.at[up + 3])
+            arrived(piece(k, y + 4, HALF), ring_sem.at[down + 3])
+            remote(inputs_t.at[c, k], inputs_t.at[c, k], core_sem.at[k], other_core)
+            return
+        lo, hi = (0, HALF) if step == 3 else (None, None)
+        remote(piece(k, y - step, lo), piece(k, y - step, lo), ring_sem.at[up + step], above)
+        remote(piece(k, y + step, hi), piece(k, y + step, hi), ring_sem.at[down + step], below)
 
     home_row = zl == src_zl
     near = 3 - 2 * zl
     groups = [jnp.where(home_row, *pair) for pair in ((0, near), (near, 0), (4 - near, 2), (2, 4 - near))]
     first_here = (True, home_row, jnp.logical_not(home_row), False)
-
-    def both(*conds):
-        return functools.reduce(jnp.logical_and, conds)
 
     def gather(n, who):
         k, first = groups[n], first_here[n]
@@ -188,9 +197,8 @@
                 if go is not None and who is is_root:
                     remote(block, block, sem, backward, go)
                 if first is not False and (who is is_root or one_row):
-                    remote(block, block, sem, other_zl, both(who, first))
-
-    is_leaf = role >= 2
+                    turn = both(who, first) if one_row else both(who, first, k != 0)
+                    remote(block, block, sem, other_zl, turn)
 
     def product(k, core):
         return lax.dot_general(
@@ -210,47 +218,44 @@
 
     def reduce(n, step):
         k = groups[n]
-        up_to, down_to = mod(y + 5 - step, NY), mod(y - 5 + step, NY)
-        up_dst, down_dst = up_in.at[k, step - 1], down_in.at[k, step - 1]
-        up_src, down_src = up_out.at[k, step - 1], down_out.at[k, step - 1]
-        lo, hi = pl.ds(0, HALF), pl.ds(HALF, HALF)
-        if step == 1:
-            up_out[k, 0, lo] = total[k, up_to, lo].astype(jnp.bfloat16)
-            down_out[k, 0, hi] = total[k, down_to, hi].astype(jnp.bfloat16)
-            up_src, up_dst = up_src.at[lo], up_dst.at[lo]
-            down_src, down_dst = down_src.at[hi], down_dst.at[hi]
-        elif step == 2:
-            arrived(up_in.at[k, 0, lo], up_sem.at[4 * k])
-            up_out[k, 1, lo] = (total[k, up_to, lo] + up_in[k, 0, lo].astype(jnp.float32)).astype(jnp.bfloat16)
-            up_out[k, 1, hi] = total[k, up_to, hi].astype(jnp.bfloat16)
-            arrived(down_in.at[k, 0, hi], down_sem.at[4 * k])
-            down_out[k, 1, hi] = (total[k, down_to, hi] + down_in[k, 0, hi].astype(jnp.float32)).astype(jnp.bfloat16)
-            down_out[k, 1, lo] = total[k, down_to, lo].astype(jnp.bfloat16)
-        else:
-            arrived(up_in.at[k, step - 2], up_sem.at[4 * k + step - 2])
-            up_out[k, step - 1] = (total[k, up_to] + up_in[k, step - 2].astype(jnp.float32)).astype(jnp.bfloat16)
-            arrived(down_in.at[k, step - 2], down_sem.at[4 * k + step - 2])
-            down_out[k, step - 1] = (total[k, down_to] + down_in[k, step - 2].astype(jnp.float32)).astype(jnp.bfloat16)
-        remote(up_src, up_dst, up_sem.at[4 * k + step - 1], above)
-        remote(down_src, down_dst, down_sem.at[4 * k + step - 1], below)
+        for turn in range(2):
+            for up in (True, False):
+                half = turn if up else 1 - turn
+                if step == 1 and turn == 1:
+                    continue
+                to = mod(y + 5 - step, NY) if up else mod(y - 5 + step, NY)
+                out, came, sem = (up_out, up_in, up_sem) if up else (down_out, down_in, down_sem)
+                rows = pl.ds(half * HALF, HALF)
+                term = total[k, to, rows]
+                if step > 2 or (step == 2 and turn == 0):
+                    arrived(came.at[k, step - 2, rows], sem.at[8 * k + 2 * (step - 2) + half])
+                    term = term + came[k, step - 2, rows].astype(jnp.float32)
+                out[k, step - 1, rows] = term.astype(jnp.bfloat16)
+                remote(
+                    out.at[k, step - 1, rows], came.at[k, step - 1, rows], sem.at[8 * k + 2 * (step - 1) + half],
+                    above if up else below,
+                )
 
     def finish(n):
         k = groups[n]
-        arrived(up_in.at[k, 3], up_sem.at[4 * k + 3])
-        arrived(down_in.at[k, 3], down_sem.at[4 * k + 3])
+        for half in range(2):
+            rows = pl.ds(half * HALF, HALF)
+            arrived(up_in.at[k, 3, rows], up_sem.at[8 * k + 6 + half])
+            arrived(down_in.at[k, 3, rows], down_sem.at[8 * k + 6 + half])
         whole = total[k, y] + up_in[k, 3].astype(jnp.float32) + down_in[k, 3].astype(jnp.float32)
         total[k, y] = whole
         z_out[k] = whole.astype(jnp.bfloat16)
         remote(z_out.at[k], z_in.at[k], z_sem.at[k], device(zh=mod(zh + k, NZ)), k != 0)
 
-    def weight_grad(k):
+    def weight_grad(n):
+        k = groups[n]
         arrived(inputs_t.at[1 - c, k], core_sem.at[k])
         for core in range(2):
             term = lax.dot_general(
                 inputs_t[core, k].reshape(FEAT, TOK), ghs[k, core], (((1,), (0,)), ((), ())),
                 preferred_element_type=jnp.float32,
             )
-            if k == 0 and core == 0:
+            if n == 0 and core == 0:
                 acc[...] = term
             else:
                 acc[...] += term
@@ -266,16 +271,16 @@
         git[...] = out.astype(jnp.bfloat16)
 
     loads[3].wait()
-    root, relay, leaf, role2, role3 = is_root, is_relay, is_leaf, role == 2, role == 3
+    root, relay, role2, role3 = is_root, is_relay, role == 2, role == 3
     schedule = (
-        (send_inputs,), (keep_hidden,), (send_hidden, far != 2), (share_inputs,), (gather, 0, root),
-        (inputs_ring, 0), (gather, 1, root), (send_hidden, both(far == 2, root)), (gather, 0, role3), (send_hidden, both(far == 2, role3)),
-        (gather, 0, relay), (inputs_ring, 1), (gather, 0, role2),
-        (compute, 0), (gather, 2, root), (gather, 1, relay), (add_pair, 0), (reduce, 0, 1), (inputs_ring, 2),
-        (gather, 3, root), (gather, 1, leaf), (compute, 1), (gather, 2, relay), (reduce, 0, 2), (inputs_ring, 3),
-        (add_pair, 1), (reduce, 1, 1), (reduce, 0, 3), (gather, 2, leaf), (compute, 2), (inputs_ring, 4),
+        (send_inputs,), (keep_hidden,), (send_hidden, far != 2, True), (share_inputs,), (gather, 0, root),
+        (inputs_ring, 0, 1), (inputs_ring, 0, 3), (inputs_ring, 0, 2), (gather, 1, root), (send_hidden, both(far == 2, root)), (gather, 0, role3), (send_hidden, both(far == 2, role3)),
+        (gather, 0, relay), (inputs_ring, 1, 1), (inputs_ring, 1, 3), (inputs_ring, 1, 2), (gather, 0, role2),
+        (compute, 0), (gather, 2, root), (gather, 1, relay), (add_pair, 0), (reduce, 0, 1), (inputs_ring, 2, 1), (inputs_ring, 2, 3), (inputs_ring, 2, 2),
+        (gather, 3, root), (gather, 1, role2), (gather, 1, role3), (compute, 1), (gather, 2, relay), (reduce, 0, 2), (inputs_ring, 3, 1), (inputs_ring, 3, 3), (inputs_ring, 3, 2),
+        (add_pair, 1), (reduce, 1, 1), (reduce, 0, 3), (gather, 2, role2), (gather, 2, role3), (compute, 2), (inputs_ring, 4, 1), (inputs_ring, 4, 3), (inputs_ring, 4, 2),
         (gather, 3, relay), (reduce, 1, 2), (reduce, 0, 4), (add_pair, 2), (reduce, 2, 1), (reduce, 1, 3),
-        (finish, 0), (gather, 3, leaf), (compute, 3), (reduce, 2, 2), (reduce, 1, 4), (add_pair, 3), (reduce, 3, 1),
+        (finish, 0), (gather, 3, role2), (gather, 3, role3), (compute, 3), (reduce, 2, 2), (reduce, 1, 4), (add_pair, 3), (reduce, 3, 1),
         (reduce, 2, 3), (finish, 1), (weight_grad, 0), (reduce, 3, 2), (reduce, 2, 4), (weight_grad, 1),
         (reduce, 3, 3), (finish, 2), (weight_grad, 2), (reduce, 3, 4), (weight_grad, 3), (write_weight_grad,),
         (finish, 3), (write_inputs_grad,),
@@ -290,7 +295,7 @@
             pl.when(cond)(copy.wait_send)
 
 
-N_SENDS = 192
+N_SENDS = 320
 
 
 def shards(grad_act, pre_act, inputs, weight):
@@ -330,8 +335,8 @@
             dma((8 * (NZ - 1),)),
             dma((NZ,)),
             dma((NZ,)),
-            dma((4 * NZ,)),
-            dma((4 * NZ,)),
+            dma((8 * NZ,)),
+            dma((8 * NZ,)),
             dma((NZ,)),
         ],
         compiler_params=pltpu.CompilerParams(

time: 93 us -> 90.7 us (0.975)
  the two profiles are of different devices: /device:TPU:64 before, /device:TPU:66 now
where the time goes in v3:
time: 90.7 us; the launch traced here: 90.4 us
  Pallas kernels  86.3 us (95%)
  local copies, waits for them, and re-layouts  3.46 us (4%)
    pallas_call x1, Pallas kernels, shards(): pl.pallas_call(kernel, out_shape=(jax.ShapeDtypeStruct((SLICE, TOK), bf16...  86.3 us
    unnamed x2, local copies, waits for them, and re-layouts  3.46 us

profile of v3, /device:TPU:66, one launch (start us, length us, event | category | flops | bytes accessed | tf_op | source)
XLA Modules:
  0.0 90.4 jit_solution(15182428125110967432)
XLA Ops:
  0.6 86.3 %shard_map.59 = (bf16[96,384]{1,0:T(8,128)(2,1)}, bf16[768,384]{1,0:T(8,128)(2,1)}) custom-call(bf16[384,384]{1,0:T(8,128)(2,1)} %ga_any.1, bf16[384,384]{1,0:T(8,128)(2,1)} %pa_any.1, bf16[384,768]{1,0:T(8,128)(2,1)} %inp_any.1, bf16[768,384]{1,0:T(8,128)(2,1)} %w_any.1), custom_call_target="tpu_custom_call" | custom-call | tf_op jit(solution)/shard_map/pallas_call | solution.py:305
  87.0 1.5 %copy.8 = bf16[384,96]{0,1:T(8,128)(2,1)} copy(bf16[384,96]{0,1:T(8,128)(2,1)} %bitcast.1) | data formatting | bytes 147456
  88.5 1.9 %copy.9 = bf16[768,384]{1,0:T(8,128)(2,1)} copy(bf16[768,384]{1,0:T(8,128)(2,1)} %get-tuple-element.9) | data formatting | bytes 1179648

commit v4 on v3

--- a/solution.py
+++ b/solution.py
@@ -200,21 +200,28 @@
                     turn = both(who, first) if one_row else both(who, first, k != 0)
                     remote(block, block, sem, other_zl, turn)
 
-    def product(k, core):
+    def product(k, core, half):
+        rows = FEAT // 2
         return lax.dot_general(
-            w[...], ghs[k, core], (((1,), (1,)), ((), ())), preferred_element_type=jnp.float32
-        ).reshape(NY, SLICE, TOK)
+            w[half * rows : (half + 1) * rows, :], ghs[k, core], (((1,), (1,)), ((), ())),
+            preferred_element_type=jnp.float32,
+        ).reshape(NY // 2, SLICE, TOK)
 
     def compute(n):
         k = groups[n]
-        pair_out[k] = product(k, 1 - c).astype(jnp.bfloat16)
-        remote(pair_out.at[k], pair_in.at[k], pair_sem.at[k], other_core)
-        total[k] = product(k, c)
+        for half in range(2):
+            some = pl.ds(half * (NY // 2), NY // 2)
+            pair_out[k, some] = product(k, 1 - c, half).astype(jnp.bfloat16)
+            remote(pair_out.at[k, some], pair_in.at[k, some], pair_sem.at[2 * k + half], other_core)
+        for half in range(2):
+            total[k, pl.ds(half * (NY // 2), NY // 2)] = product(k, c, half)
 
     def add_pair(n):
         k = groups[n]
-        arrived(pair_in.at[k], pair_sem.at[k])
-        total[k] = total[k] + pair_in[k].astype(jnp.float32)
+        for half in range(2):
+            some = pl.ds(half * (NY // 2), NY // 2)
+            arrived(pair_in.at[k, some], pair_sem.at[2 * k + half])
+            total[k, some] = total[k, some] + pair_in[k, some].astype(jnp.float32)
 
     def reduce(n, step):
         k = groups[n]
@@ -334,7 +341,7 @@
             dma((NZ - 1,)),
             dma((8 * (NZ - 1),)),
             dma((NZ,)),
-            dma((NZ,)),
+            dma((2 * NZ,)),
             dma((8 * NZ,)),
             dma((8 * NZ,)),
             dma((NZ,)),

time: 90.7 us -> 91.7 us (1.011)
  the two profiles are of different devices: /device:TPU:66 before, /device:TPU:64 now
where the time goes in v4:
time: 91.7 us; the launch traced here: 91.4 us
  Pallas kernels  87.3 us (95%)
  local copies, waits for them, and re-layouts  3.46 us (4%)
    pallas_call x1, Pallas kernels, shards(): pl.pallas_call(kernel, out_shape=(jax.ShapeDtypeStruct((SLICE, TOK), bf16...  87.3 us
    unnamed x2, local copies, waits for them, and re-layouts  3.46 us

profile of v4, /device:TPU:64, one launch (start us, length us, event | category | flops | bytes accessed | tf_op | source)
XLA Modules:
  0.0 91.4 jit_solution(14679071168874526560)
XLA Ops:
  0.6 87.3 %shard_map.59 = (bf16[96,384]{1,0:T(8,128)(2,1)}, bf16[768,384]{1,0:T(8,128)(2,1)}) custom-call(bf16[384,384]{1,0:T(8,128)(2,1)} %ga_any.1, bf16[384,384]{1,0:T(8,128)(2,1)} %pa_any.1, bf16[384,768]{1,0:T(8,128)(2,1)} %inp_any.1, bf16[768,384]{1,0:T(8,128)(2,1)} %w_any.1), custom_call_target="tpu_custom_call" | custom-call | tf_op jit(solution)/shard_map/pallas_call | solution.py:312
  88.0 1.5 %copy.8 = bf16[384,96]{0,1:T(8,128)(2,1)} copy(bf16[384,96]{0,1:T(8,128)(2,1)} %bitcast.1) | data formatting | bytes 147456
  89.5 1.9 %copy.9 = bf16[768,384]{1,0:T(8,128)(2,1)} copy(bf16[768,384]{1,0:T(8,128)(2,1)} %get-tuple-element.9) | data formatting | bytes 1179648

commit v5 on v3

--- a/solution.py
+++ b/solution.py
@@ -218,30 +218,34 @@
 
     def reduce(n, step):
         k = groups[n]
-        for turn in range(2):
-            for up in (True, False):
-                half = turn if up else 1 - turn
-                if step == 1 and turn == 1:
-                    continue
-                to = mod(y + 5 - step, NY) if up else mod(y - 5 + step, NY)
-                out, came, sem = (up_out, up_in, up_sem) if up else (down_out, down_in, down_sem)
-                rows = pl.ds(half * HALF, HALF)
-                term = total[k, to, rows]
-                if step > 2 or (step == 2 and turn == 0):
-                    arrived(came.at[k, step - 2, rows], sem.at[8 * k + 2 * (step - 2) + half])
-                    term = term + came[k, step - 2, rows].astype(jnp.float32)
-                out[k, step - 1, rows] = term.astype(jnp.bfloat16)
-                remote(
-                    out.at[k, step - 1, rows], came.at[k, step - 1, rows], sem.at[8 * k + 2 * (step - 1) + half],
-                    above if up else below,
-                )
+        up_to, down_to = mod(y + 5 - step, NY), mod(y - 5 + step, NY)
+        up_dst, down_dst = up_in.at[k, step - 1], down_in.at[k, step - 1]
+        up_src, down_src = up_out.at[k, step - 1], down_out.at[k, step - 1]
+        lo, hi = pl.ds(0, HALF), pl.ds(HALF, HALF)
+        if step == 1:
+            up_out[k, 0, lo] = total[k, up_to, lo].astype(jnp.bfloat16)
+            down_out[k, 0, hi] = total[k, down_to, hi].astype(jnp.bfloat16)
+            up_src, up_dst = up_src.at[lo], up_dst.at[lo]
+            down_src, down_dst = down_src.at[hi], down_dst.at[hi]
+        elif step == 2:
+            arrived(up_in.at[k, 0, lo], up_sem.at[4 * k])
+            up_out[k, 1, lo] = (total[k, up_to, lo] + up_in[k, 0, lo].astype(jnp.float32)).astype(jnp.bfloat16)
+            up_out[k, 1, hi] = total[k, up_to, hi].astype(jnp.bfloat16)
+            arrived(down_in.at[k, 0, hi], down_sem.at[4 * k])
+            down_out[k, 1, hi] = (total[k, down_to, hi] + down_in[k, 0, hi].astype(jnp.float32)).astype(jnp.bfloat16)
+            down_out[k, 1, lo] = total[k, down_to, lo].astype(jnp.bfloat16)
+        else:
+            arrived(up_in.at[k, step - 2], up_sem.at[4 * k + step - 2])
+            up_out[k, step - 1] = (total[k, up_to] + up_in[k, step - 2].astype(jnp.float32)).astype(jnp.bfloat16)
+            arrived(down_in.at[k, step - 2], down_sem.at[4 * k + step - 2])
+            down_out[k, step - 1] = (total[k, down_to] + down_in[k, step - 2].astype(jnp.float32)).astype(jnp.bfloat16)
+        remote(up_src, up_dst, up_sem.at[4 * k + step - 1], above)
+        remote(down_src, down_dst, down_sem.at[4 * k + step - 1], below)
 
     def finish(n):
         k = groups[n]
-        for half in range(2):
-            rows = pl.ds(half * HALF, HALF)
-            arrived(up_in.at[k, 3, rows], up_sem.at[8 * k + 6 + half])
-            arrived(down_in.at[k, 3, rows], down_sem.at[8 * k + 6 + half])
+        arrived(up_in.at[k, 3], up_sem.at[4 * k + 3])
+        arrived(down_in.at[k, 3], down_sem.at[4 * k + 3])
         whole = total[k, y] + up_in[k, 3].astype(jnp.float32) + down_in[k, 3].astype(jnp.float32)
         total[k, y] = whole
         z_out[k] = whole.astype(jnp.bfloat16)

time: 90.7 us -> 93.9 us (1.035)
  the two profiles are of different devices: /device:TPU:66 before, /device:TPU:64 now
where the time goes in v5:
time: 93.9 us; the launch traced here: 93.7 us
  Pallas kernels  89.6 us (95%)
  local copies, waits for them, and re-layouts  3.46 us (4%)
    pallas_call x1, Pallas kernels, shards(): pl.pallas_call(kernel, out_shape=(jax.ShapeDtypeStruct((SLICE, TOK), bf16...  89.6 us
    unnamed x2, local copies, waits for them, and re-layouts  3.46 us

profile of v5, /device:TPU:64, one launch (start us, length us, event | category | flops | bytes accessed | tf_op | source)
XLA Modules:
  0.0 93.7 jit_solution(1373497976119595574)
XLA Ops:
  0.6 89.6 %shard_map.59 = (bf16[96,384]{1,0:T(8,128)(2,1)}, bf16[768,384]{1,0:T(8,128)(2,1)}) custom-call(bf16[384,384]{1,0:T(8,128)(2,1)} %ga_any.1, bf16[384,384]{1,0:T(8,128)(2,1)} %pa_any.1, bf16[384,768]{1,0:T(8,128)(2,1)} %inp_any.1, bf16[768,384]{1,0:T(8,128)(2,1)} %w_any.1), custom_call_target="tpu_custom_call" | custom-call | tf_op jit(solution)/shard_map/pallas_call | solution.py:309
  90.3 1.5 %copy.8 = bf16[384,96]{0,1:T(8,128)(2,1)} copy(bf16[384,96]{0,1:T(8,128)(2,1)} %bitcast.1) | data formatting | bytes 147456
  91.8 1.9 %copy.9 = bf16[768,384]{1,0:T(8,128)(2,1)} copy(bf16[768,384]{1,0:T(8,128)(2,1)} %get-tuple-element.9) | data formatting | bytes 1179648
